TPU v7x, 256 devices: a whole 4x4x8 slice. The times are simulated.
256 devices in a mesh: seq: 32 (over z, y), head: 8 (over x, core).
Axes of the slice: x: 4, y: 4, z: 8, core: 2. Of those that a mesh axis runs over, the one named last changes fastest.
Arguments:
- query_rows: bfloat16 [65536, 4096], P(('seq', 'head')), may hold values from -6 to 6
- key_rows: bfloat16 [65536, 4096], P(('seq', 'head')), may hold values from -6 to 6
- value_rows: bfloat16 [65536, 4096], P(('seq', 'head')), may hold values from -6 to 6
- norm_gain: float32 [4096], P('head'), may hold values from 0.1 to 1.9
Outputs:
- mixed: bfloat16 [65536, 4096], P('seq', 'head')
All inputs are finite; a program needn't handle non-finite values.
Results may differ from a plain program's by a relative error of at most 0.0027.
Values may be sent and summed in bfloat16 or wider, within the bound.
A program may use at most 128 MiB of HBM per device.

v0:
```python
import jax
import jax.numpy as jnp
from jax import lax
from jax.sharding import PartitionSpec as P

E = 128
BLOCK = 512


def entering(value, axis, combine, identity):
    length, place = (lax.axis_size(axis), lax.axis_index(axis))
    everything = lax.all_gather(value, axis)
    start = jnp.broadcast_to(jnp.asarray(identity, value.dtype), value.shape)

    def hop(k, before):
        reached = k < place
        new = combine(before, everything[k])
        return jnp.where(reached, new, before)

    return lax.fori_loop(0, length, hop, start)


def combine_sum(earlier, later):
    return earlier + later


def prefix_states(own_state):
    return entering(own_state, "seq", combine_sum, jnp.zeros_like(own_state))


def local_state(key_heads, value_heads):
    return jnp.einsum("the,thf->hef", key_heads, value_heads, preferred_element_type=jnp.float32)


def attend(query_heads, key_heads, value_heads, start_state):
    tokens_here, heads_here, width = query_heads.shape
    blocks = tokens_here // BLOCK
    query_blocks = query_heads.reshape(blocks, BLOCK, heads_here, width)
    key_blocks = key_heads.reshape(blocks, BLOCK, heads_here, width)
    value_blocks = value_heads.reshape(blocks, BLOCK, heads_here, width)
    rowpos = lax.broadcasted_iota(jnp.int32, (BLOCK, BLOCK), 0)
    colpos = lax.broadcasted_iota(jnp.int32, (BLOCK, BLOCK), 1)
    causal = colpos <= rowpos

    def advance(running, pieces):
        query_blk, key_blk, value_blk = pieces
        scores = jnp.einsum("bhe,che->hbc", query_blk, key_blk, preferred_element_type=jnp.float32)
        weights = jnp.where(causal[None], scores, 0.0).astype(jnp.bfloat16)
        within = jnp.einsum("hbc,che->bhe", weights, value_blk, preferred_element_type=jnp.float32)
        carried = jnp.einsum(
            "bhe,hef->bhf", query_blk.astype(jnp.float32), running, precision=lax.Precision.HIGHEST
        )
        running = running + jnp.einsum(
            "bhe,bhf->hef", key_blk, value_blk, preferred_element_type=jnp.float32
        )
        return (running, carried + within)

    _, attended = lax.scan(advance, start_state, (query_blocks, key_blocks, value_blocks))
    return attended.reshape(tokens_here, heads_here, width)


def shards(query_rows, key_rows, value_rows, norm_gain):
    width = E
    query_local, key_local, value_local = (
        lax.all_to_all(query_rows, "head", split_axis=1, concat_axis=0, tiled=True),
        lax.all_to_all(key_rows, "head", split_axis=1, concat_axis=0, tiled=True),
        lax.all_to_all(value_rows, "head", split_axis=1, concat_axis=0, tiled=True),
    )
    tokens_here = query_local.shape[0]
    heads_here = query_local.shape[1] // width
    key_heads = key_local.reshape(tokens_here, heads_here, width)
    value_heads = value_local.reshape(tokens_here, heads_here, width)
    start_state = prefix_states(local_state(key_heads, value_heads))
    query_heads = query_local.reshape(tokens_here, heads_here, width)
    attended = attend(query_heads, key_heads, value_heads, start_state)
    scale_rms = jnp.sqrt(jnp.mean(attended * attended, axis=-1, keepdims=True) + 1e-06)
    normed = (attended / scale_rms).reshape(tokens_here, heads_here * width) * norm_gain
    return normed.astype(jnp.bfloat16)


def solution(mesh):
    placed = (
        P(("seq", "head"), None),
        P(("seq", "head"), None),
        P(("seq", "head"), None),
        P("head"),
    )
    return jax.shard_map(
        shards, mesh=mesh, in_specs=placed, out_specs=P("seq", "head"), check_vma=False
    )
```

profile of v0, /device:TPU:1, one launch (start us, length us, event | category | flops | bytes accessed | tf_op | source)
XLA Modules:
  0.0 262.8 jit_solution(10307462549238607121)
XLA Ops:
  6.5 3.1 %copy.82 = bf16[32,8,8,512]{3,2,0,1:T(8,128)(2,1)} copy(bf16[32,8,8,512]{3,2,1,0:T(8,128)(2,1)} %bitcast.89) | data formatting | bytes 4194304 | tf_op jit(solution)/shard_map/all_to_all | solution.py:66
  9.7 6.7 %all-to-all-start = ((bf16[256,8,512]{2,0,1:T(8,128)(2,1)}), bf16[256,8,512]{2,0,1:T(8,128)(2,1)S(1)}, u32[]{:S(2)}, u32[]{:S(2)}) async-start(bf16[256,8,512]{2,0,1:T(8,128)(2,1)} %bitcast.88), calls=%async_computation | async-start | bytes 4194304 | tf_op jit(solution)/shard_map/all_to_all | solution.py:66
  16.4 3.1 %copy.81 = bf16[32,8,8,512]{3,2,0,1:T(8,128)(2,1)} copy(bf16[32,8,8,512]{3,2,1,0:T(8,128)(2,1)} %bitcast.90) | data formatting | bytes 4194304 | tf_op jit(solution)/shard_map/all_to_all | solution.py:67
  19.5 23.2 %all-to-all-done = bf16[256,8,512]{2,0,1:T(8,128)(2,1)S(1)} async-done(((bf16[256,8,512]{2,0,1:T(8,128)(2,1)}), bf16[256,8,512]{2,0,1:T(8,128)(2,1)S(1)}, u32[]{:S(2)}, u32[]{:S(2)}) %all-to-all-start) | async-done | bytes 2097184 | tf_op jit(solution)/shard_map/all_to_all | solution.py:66
  42.8 5.1 %all-to-all-start.1 = ((bf16[256,8,512]{2,0,1:T(8,128)(2,1)}), bf16[256,8,512]{2,0,1:T(8,128)(2,1)}, u32[]{:S(2)}, u32[]{:S(2)}) async-start(bf16[256,8,512]{2,0,1:T(8,128)(2,1)} %bitcast.87), calls=%async_computation.1 | async-start | bytes 4194304 | tf_op jit(solution)/shard_map/all_to_all | solution.py:67
  47.9 2.1 reshape.49
  49.9 24.4 %all-to-all-done.1 = bf16[256,8,512]{2,0,1:T(8,128)(2,1)} async-done(((bf16[256,8,512]{2,0,1:T(8,128)(2,1)}), bf16[256,8,512]{2,0,1:T(8,128)(2,1)}, u32[]{:S(2)}, u32[]{:S(2)}) %all-to-all-start.1) | async-done | bytes 2097184 | tf_op jit(solution)/shard_map/all_to_all | solution.py:67
  74.3 4.0 %reshape.50 = bf16[2048,4,128]{2,1,0:T(4,128)(2,1)} reshape(bf16[8,256,512]{2,1,0:T(8,128)(2,1)} %bitcast.1) | data formatting | bytes 4194304 | tf_op jit(solution)/shard_map/reshape | solution.py:72
  78.3 3.9 %fusion.13 = f32[4,128,128]{2,1,0:T(8,128)} fusion(bf16[2048,4,128]{2,1,0:T(4,128)(2,1)} %reshape.50, bf16[2048,4,128]{2,1,0:T(4,128)(2,1)} %reshape.49), kind=kOutput, calls=%fused_computation.26 | convolution fusion | flops 268435456 | bytes 4456448 | tf_op jit(solution)/shard_map/the,thf->hef/dot_general | solution.py:32
  82.2 3.1 %copy.80 = bf16[32,8,8,512]{3,2,0,1:T(8,128)(2,1)} copy(bf16[32,8,8,512]{3,2,1,0:T(8,128)(2,1)} %bitcast.91) | data formatting | bytes 4194304 | tf_op jit(solution)/shard_map/all_to_all | solution.py:65
  85.3 5.1 %all-to-all-start.2 = ((bf16[256,8,512]{2,0,1:T(8,128)(2,1)}), bf16[256,8,512]{2,0,1:T(8,128)(2,1)}, u32[]{:S(2)}, u32[]{:S(2)}) async-start(bf16[256,8,512]{2,0,1:T(8,128)(2,1)} %bitcast.86), calls=%async_computation.2 | async-start | bytes 4194304 | tf_op jit(solution)/shard_map/all_to_all | solution.py:65
  90.4 4.0 %reshape_reshape.10 = bf16[4,512,4,128]{3,2,1,0:T(4,128)(2,1)} reshape(bf16[8,256,512]{2,1,0:T(8,128)(2,1)} %bitcast.1) | data formatting | bytes 4194304 | tf_op jit(solution)/shard_map/reshape;reshape | solution.py:40
  94.4 2.0 reshape_reshape.9
  96.4 20.5 %all-to-all-done.2 = bf16[256,8,512]{2,0,1:T(8,128)(2,1)} async-done(((bf16[256,8,512]{2,0,1:T(8,128)(2,1)}), bf16[256,8,512]{2,0,1:T(8,128)(2,1)}, u32[]{:S(2)}, u32[]{:S(2)}) %all-to-all-start.2) | async-done | bytes 2097184 | tf_op jit(solution)/shard_map/all_to_all | solution.py:65
  116.8 4.0 %reshape_reshape.11 = bf16[4,512,4,128]{3,2,1,0:T(4,128)(2,1)} reshape(bf16[8,256,512]{2,1,0:T(8,128)(2,1)} %bitcast.3) | data formatting | bytes 4194304 | tf_op jit(solution)/shard_map/reshape;reshape | solution.py:38
  120.8 59.8 %all-gather.3.cloned.1.call-done = f32[128,128,128]{2,1,0:T(8,128)} async-done(((f32[4,128,128]{2,1,0:T(8,128)}), f32[128,128,128]{2,1,0:T(8,128)}) %all-gather.3.cloned.1.call-update) | async-done | bytes 8388624 | tf_op jit(solution)/shard_map/all_gather | solution.py:12
  180.6 34.0 %while.28 = (s32[]{:T(128)}, f32[4,128,128]{2,1,0:T(8,128)S(1)}, s32[]{:T(128)}, f32[32,4,128,128]{3,2,1,0:T(8,128)}, s32[]{:T(128)}, /*index=5*/s32[]{:T(128)}) while((s32[]{:T(128)}, f32[4,128,128]{2,1,0:T(8,128)S(1)}, s32[]{:T(128)}, f32[32,4,128,128]{3,2,1,0:T(8,128)}, s32[]{:T(128)}, /*index=5*/s32[]{:T(128)}) %tuple.62), condition=%wide.region_1.2_spmd.clone, body=%wide.region_0.1_spmd.clone.sunk | while | flops 196612 | bytes 786525 | solution.py:20
  214.7 25.5 %while.27 = (s32[]{:T(128)}, f32[4,128,128]{2,1,0:T(8,128)S(1)}, f32[4,512,4,128]{3,1,2,0:T(8,128)}, bf16[4,512,4,128]{3,2,1,0:T(4,128)(2,1)}, bf16[4,512,4,128]...) while((s32[]{:T(128)}, f32[4,128,128]{2,1,0:T(8,128)S(1)}, ...), condition=%wide.region_3.4_spmd.clone, body=%wide.region_2.3_spmd.clone.sunk | while | flops 1009319936 | bytes 11797077 | solution.py:58
  214.7 1.6 constant_dynamic-slice_fusion.6
  216.8 1.2 constant_dynamic-slice_fusion.5
  218.5 2.3 fusion.24
  221.1 1.6 constant_dynamic-slice_fusion.6
  223.2 1.2 constant_dynamic-slice_fusion.5
  224.9 2.2 fusion.24
  227.4 1.6 constant_dynamic-slice_fusion.6
  231.2 2.3 fusion.24
  233.8 1.6 constant_dynamic-slice_fusion.6
  237.6 2.2 fusion.24
  240.1 3.5 %multiply_reduce_fusion = f32[4,512,4]{1,2,0:T(4,128)S(1)} fusion(f32[4,512,4,128]{3,1,2,0:T(8,128)} %get-tuple-element.122), kind=kLoop, calls=%fused_computation.22 | loop fusion | flops 2088960 | bytes 4227072 | tf_op jit(solution)/shard_map/reduce_sum | solution.py:76
  243.7 4.6 %copy.46 = f32[4,512,4,128]{3,2,1,0:T(4,128)} copy(f32[4,512,4,128]{3,1,2,0:T(8,128)S(1)} %copy-done) | data formatting | bytes 8388608 | tf_op jit(solution)/shard_map/while | solution.py:58
  248.7 4.7 %div.19 = f32[2048,4,128]{2,1,0:T(4,128)S(1)} broadcast(f32[2048,4]{1,0:T(8,128)S(1)} %copy.47), dimensions={0,1} | broadcast | bytes 4227072 | tf_op jit(solution)/shard_map/div | solution.py:77
  253.4 2.5 fusion.12
  (62 shorter events, 41.3 us)
Async XLA Ops:
  9.7 33.1 %all-to-all-start = ((bf16[256,8,512]{2,0,1:T(8,128)(2,1)}), bf16[256,8,512]{2,0,1:T(8,128)(2,1)S(1)}, u32[]{:S(2)}, u32[]{:S(2)}) async-start(bf16[256,8,512]{2,0,1:T(8,128)(2,1)} %bitcast.88), calls=%async_computation | async-start | bytes 4194304 | tf_op jit(solution)/shard_map/all_to_all | solution.py:66
  42.8 31.6 %all-to-all-start.1 = ((bf16[256,8,512]{2,0,1:T(8,128)(2,1)}), bf16[256,8,512]{2,0,1:T(8,128)(2,1)}, u32[]{:S(2)}, u32[]{:S(2)}) async-start(bf16[256,8,512]{2,0,1:T(8,128)(2,1)} %bitcast.87), calls=%async_computation.1 | async-start | bytes 4194304 | tf_op jit(solution)/shard_map/all_to_all | solution.py:67
  47.9 132.8 %all-gather.3.cloned.1.call-start = ((), (), s32[]{:S(2)}) async-start(), calls=%async_computation.3 | async-start | bytes 8650752 | tf_op jit(solution)/shard_map/all_gather | solution.py:12
  85.3 31.6 %all-to-all-start.2 = ((bf16[256,8,512]{2,0,1:T(8,128)(2,1)}), bf16[256,8,512]{2,0,1:T(8,128)(2,1)}, u32[]{:S(2)}, u32[]{:S(2)}) async-start(bf16[256,8,512]{2,0,1:T(8,128)(2,1)} %bitcast.86), calls=%async_computation.2 | async-start | bytes 4194304 | tf_op jit(solution)/shard_map/all_to_all | solution.py:65
  240.1 3.5 %copy-start = (f32[4,512,4,128]{3,1,2,0:T(8,128)S(1)}, f32[4,512,4,128]{3,1,2,0:T(8,128)}, u32[]{:S(2)}) copy-start(f32[4,512,4,128]{3,1,2,0:T(8,128)} %get-tuple-element.122) | copy-start | bytes 12582916
  248.7 4.7 %copy-start.1 = (f32[4,512,4,128]{3,2,1,0:T(4,128)S(1)}, f32[4,512,4,128]{3,2,1,0:T(4,128)}, u32[]{:S(2)}) copy-start(f32[4,512,4,128]{3,2,1,0:T(4,128)} %copy.46) | copy-start | bytes 12582916
  248.7 4.7 %copy-start.2 = (f32[512]{0:T(512)S(1)}, f32[512]{0:T(512)}, u32[]{:S(2)}) copy-start(f32[512]{0:T(512)} %param.11) | copy-start | bytes 6148
Sparse Core Ops, SparseCore 0:
  82.3 98.2 all-gather.2
where the time goes:
time: 265 us; the launch traced here: 263 us
  waiting for transfers between devices  128 us (48%)
  local copies, waits for them, and re-layouts  47.5 us (18%)
  other arithmetic  39.6 us (15%)
  starting transfers between devices  17 us (6%)
  matrix products  16.4 us (6%)
  between operations  13.5 us (5%)
    all_gather x1, waiting for transfers between devices, entering(): everything = lax.all_gather(value, axis)  59.8 us
    select_n x32, other arithmetic, hop(): return jnp.where(reached, new, before)  33.3 us
    all_to_all x1, waiting for transfers between devices, shards(): lax.all_to_all(value_rows, 'head', split_axis=1, concat_axis=0, tiled=True)  24.4 us
    all_to_all x1, waiting for transfers between devices, shards(): lax.all_to_all(key_rows, 'head', split_axis=1, concat_axis=0, tiled=True)  23.2 us
    all_to_all x1, waiting for transfers between devices, shards(): lax.all_to_all(query_rows, 'head', split_axis=1, concat_axis=0, tiled=True)  20.5 us
    dynamic_slice x12, local copies, waits for them, and re-layouts, attend(): lax.scan(advance, start_state, (query_blocks, key_blocks, value_blocks))  12.5 us
    dot_general x4, matrix products, advance(): jnp.einsum('hbc,che->bhe', weights, value_blk, preferred_element_type=jnp...  9.01 us
    all_to_all x1, starting transfers between devices, shards(): lax.all_to_all(key_rows, 'head', split_axis=1, concat_axis=0, tiled=True)  6.74 us
  transfers between devices with their start and end apart: 4, of which 4 were waited for; matrix products, arithmetic and copies ran while one was open for 7% of the time, Pallas kernels for 0%

commit v1 on v0

v1 whole, which is shorter than its diff:
```python
import functools

import jax
import jax.numpy as jnp
from jax import lax
from jax.experimental import pallas as pl
from jax.experimental.pallas import tpu as pltpu
from jax.sharding import PartitionSpec as P

E = 128
TOKENS = 256
NX, NY, NZ, CORES = 4, 4, 8, 2
CHIPS = NX * NY
GROUP = NX * CORES
SETS = 2
PIECE = E // 2
STEPS = 4
SCALE = 1024.0
MESH = pl.DeviceIdType.MESH


def encode(state):
    scaled = state * SCALE
    return ((scaled * jnp.abs(scaled)) * (scaled * scaled)).astype(jnp.bfloat16)


def decode(code):
    wide = code.astype(jnp.float32)
    root = lax.rsqrt(lax.rsqrt(jnp.abs(wide))) * (1.0 / SCALE)
    return jnp.where(wide < 0.0, -root, root)


def kernel(q_hbm, k_hbm, v_hbm, gain_ref, out_hbm,
           q, k, v, own, sib, within, coded, landed, ahead, zcode, zland, pcode, pstate, result, gmine, gall,
           load_sem, sib_send, sib_recv, fwd_send, fwd_recv, z_send, z_recv, back_send, back_recv,
           pair_send, pair_recv, out_send, out_recv, gain_send, gain_recv):
    seq, me = lax.axis_index("seq"), lax.axis_index("head")
    z, y = lax.div(seq, NY), lax.rem(seq, NY)
    x, c = lax.div(me, CORES), lax.rem(me, CORES)
    n = y * NX + x

    def chip(a):
        return (z * NY + lax.div(a, NX), lax.rem(a, NX) * CORES + c)

    def depth(step):
        return (lax.rem(z + step, NZ) * NY + y, me)

    other = (seq, x * CORES + 1 - c)

    def turned(i):
        return lax.rem(n + 1 + i, CHIPS)

    def columns(h):
        return pl.ds(pl.multiple_of(h * E, E), E)

    def head_of(s, a):
        return 4 * lax.div(a, 2) + 2 * s + lax.rem(a, 2)

    half = pl.ds(pl.multiple_of(c * PIECE, PIECE), PIECE)

    loads = [
        pltpu.make_async_copy(src, dst, load_sem.at[i])
        for i, (src, dst) in enumerate(((k_hbm, k), (v_hbm, v), (q_hbm, q)))
    ]
    for load in loads:
        load.start()

    barrier = pltpu.get_barrier_semaphore()

    @pl.loop(1, CHIPS)
    def _(i):
        pl.semaphore_signal(barrier, inc=1, device_id=chip(lax.rem(n + i, CHIPS)), device_id_type=MESH)

    @pl.loop(1, NZ)
    def _(i):
        pl.semaphore_signal(barrier, inc=1, device_id=depth(i), device_id_type=MESH)

    @pl.loop(0, NX)
    def _(i):
        pl.semaphore_signal(
            barrier, inc=1, device_id=(seq, lax.rem(x + i, NX) * CORES + 1 - c), device_id_type=MESH
        )

    loads[0].wait()
    loads[1].wait()

    def sib_copy(s, g):
        part = pl.ds(g * STEPS, STEPS)
        return pltpu.make_async_remote_copy(
            own.at[s, part], sib.at[s, part], sib_send.at[s, g], sib_recv.at[s, g],
            device_id=other, device_id_type=MESH,
        )

    def outer(s, i):
        col = columns(head_of(s, turned(i)))
        own[s, i] = lax.dot_general(
            k[:, col], v[:, col], (((0,), (0,)), ((), ())), preferred_element_type=jnp.float32
        )

    @pl.loop(0, STEPS)
    def _(i):
        outer(0, i)

    pl.semaphore_wait(barrier, CHIPS - 1 + NZ - 1 + NX)
    sib_copy(0, 0).start()

    for s in range(SETS):
        @pl.loop(1 if s == 0 else 0, CHIPS // STEPS)
        def _(g):
            @pl.loop(0, STEPS)
            def _(u):
                outer(s, g * STEPS + u)
            sib_copy(s, g).start()

    def gain_copy(i):
        j = lax.rem(me + i, GROUP)
        return pltpu.make_async_remote_copy(
            gmine, gall.at[me], gain_send.at[i], gain_recv.at[me], device_id=(seq, j), device_id_type=MESH
        )

    def gain_landing(i):
        j = lax.rem(me + i, GROUP)
        return pltpu.make_async_remote_copy(
            gmine, gall.at[j], gain_send.at[i], gain_recv.at[j], device_id=(seq, j), device_id_type=MESH
        )

    def fwd_copy(s, i):
        return pltpu.make_async_remote_copy(
            coded.at[s, i], landed.at[s, n], fwd_send.at[s, i], fwd_recv.at[s, n],
            device_id=chip(turned(i)), device_id_type=MESH,
        )

    def fwd_landing(s, a):
        return pltpu.make_async_remote_copy(
            coded.at[s, 0], landed.at[s, a], fwd_send.at[s, 0], fwd_recv.at[s, a],
            device_id=chip(a), device_id_type=MESH,
        )

    def z_copy(s, i):
        return pltpu.make_async_remote_copy(
            zcode.at[s], zland.at[s, z], z_send.at[s, i], z_recv.at[s, z],
            device_id=depth(i), device_id_type=MESH,
        )

    def z_landing(s, i):
        origin = lax.rem(z + i, NZ)
        return pltpu.make_async_remote_copy(
            zcode.at[s], zland.at[s, origin], z_send.at[s, i], z_recv.at[s, origin],
            device_id=depth(i), device_id_type=MESH,
        )

    def back_copy(s, i):
        return pltpu.make_async_remote_copy(
            pcode.at[s, i], pstate.at[s, c, n], back_send.at[s, i], back_recv.at[s, n],
            device_id=chip(turned(i)), device_id_type=MESH,
        )

    def back_landing(s, a):
        return pltpu.make_async_remote_copy(
            pcode.at[s, 0], pstate.at[s, c, a], back_send.at[s, 0], back_recv.at[s, a],
            device_id=chip(a), device_id_type=MESH,
        )

    def pair_copy(s, which):
        return pltpu.make_async_remote_copy(
            pstate.at[s, which], pstate.at[s, which], pair_send.at[s], pair_recv.at[s],
            device_id=other, device_id_type=MESH,
        )

    def out_copy(s, t):
        return pltpu.make_async_remote_copy(
            result.at[s, t],
            out_hbm.at[pl.ds(pl.multiple_of(me * TOKENS, TOKENS), TOKENS), pl.ds(s * 2 * E, 2 * E)],
            out_send.at[s, t], out_recv.at[s, me],
            device_id=(seq, lax.rem(me + 1 + t, GROUP)), device_id_type=MESH,
        )

    def out_landing(s, t):
        j = lax.rem(me + 1 + t, GROUP)
        return pltpu.make_async_remote_copy(
            result.at[s, t],
            out_hbm.at[pl.ds(pl.multiple_of(j * TOKENS, TOKENS), TOKENS), pl.ds(s * 2 * E, 2 * E)],
            out_send.at[s, t], out_recv.at[s, j],
            device_id=(seq, j), device_id_type=MESH,
        )

    def out_local(s):
        return pltpu.make_async_copy(
            result.at[s, GROUP - 1],
            out_hbm.at[pl.ds(pl.multiple_of(me * TOKENS, TOKENS), TOKENS), pl.ds(s * 2 * E, 2 * E)],
            out_send.at[s, GROUP - 1],
        )

    for s in range(SETS):
        @pl.loop(0, CHIPS // STEPS)
        def _(g):
            sib_copy(s, g).wait_recv()

            @pl.loop(0, STEPS)
            def _(u):
                i = g * STEPS + u
                coded[s, i] = encode(own[s, i, half, :] + sib[s, i, half, :])

                @pl.when(i < CHIPS - 1)
                def _():
                    fwd_copy(s, i).start()

                @pl.when(i == CHIPS - 1)
                def _():
                    landed[s, n] = coded[s, i]

    gmine[...] = jnp.broadcast_to(gain_ref[...], gmine.shape)
    gall[me] = jnp.broadcast_to(gain_ref[...], gmine.shape)

    @pl.loop(1, GROUP)
    def _(i):
        gain_copy(i).start()

    loads[2].wait()
    causal = lax.broadcasted_iota(jnp.int32, (TOKENS, TOKENS), 1) <= lax.broadcasted_iota(
        jnp.int32, (TOKENS, TOKENS), 0
    )

    def inside(h):
        col = columns(h)
        scores = lax.dot_general(
            q[:, col], k[:, col], (((1,), (1,)), ((), ())), preferred_element_type=jnp.float32
        )
        weights = jnp.where(causal, scores, 0.0).astype(jnp.bfloat16)
        within[h] = jnp.dot(weights, v[:, col], preferred_element_type=jnp.float32)

    def inside_part(first, last):
        @pl.loop(first, last)
        def _(h):
            inside(h)

    def gather_plane(s):
        @pl.loop(1, CHIPS)
        def _(i):
            fwd_landing(s, lax.rem(n + CHIPS - i, CHIPS)).wait_recv()

        def add(a, total):
            ahead[s, a] = total
            return total + decode(landed[s, a])

        total = lax.fori_loop(0, CHIPS, add, jnp.zeros((PIECE, E), jnp.float32))
        zcode[s] = encode(total)

        @pl.loop(1, NZ)
        def _(i):
            z_copy(s, i).start()

    def give_back(s):
        def add(i, base):
            origin = lax.rem(z + i, NZ)
            z_landing(s, i).wait_recv()
            return base + jnp.where(origin < z, decode(zland[s, origin]), 0.0)

        base = lax.fori_loop(1, NZ, add, jnp.zeros((PIECE, E), jnp.float32))

        @pl.loop(0, CHIPS)
        def _(i):
            pcode[s, i] = encode(base + ahead[s, turned(i)])

            @pl.when(i < CHIPS - 1)
            def _():
                back_copy(s, i).start()

            @pl.when(i == CHIPS - 1)
            def _():
                pstate[s, c, n] = pcode[s, i]

    def share(s):
        @pl.loop(1, CHIPS)
        def _(i):
            back_landing(s, lax.rem(n + CHIPS - i, CHIPS)).wait_recv()
        pair_copy(s, c).start()

    def finish(s):
        pair_copy(s, 1 - c).wait_recv()

        @pl.loop(0, GROUP)
        def _(t):
            j = lax.rem(me + 1 + t, GROUP)
            for u in range(2):
                a = 2 * j + u
                h = 4 * j + 2 * s + u
                col = columns(h)
                before = jnp.concatenate([decode(pstate[s, 0, a]), decode(pstate[s, 1, a])], axis=0)
                beside = sib[s, lax.rem(a - n - 1 + CHIPS, CHIPS)]
                before = before + jnp.where(c == 1, beside, 0.0)
                high = before.astype(jnp.bfloat16)
                low = (before - high.astype(jnp.float32)).astype(jnp.bfloat16)
                queries = q[:, col]
                attended = (
                    within[h]
                    + jnp.dot(queries, high, preferred_element_type=jnp.float32)
                    + jnp.dot(queries, low, preferred_element_type=jnp.float32)
                )
                mean = jnp.mean(attended * attended, axis=-1, keepdims=True)
                gain = gall[j, 0:1, (2 * s + u) * E:(2 * s + u + 1) * E]
                normed = attended * lax.rsqrt(mean + 1e-06) * gain
                result[s, t, :, u * E:(u + 1) * E] = normed.astype(jnp.bfloat16)

            @pl.when(t < GROUP - 1)
            def _():
                out_copy(s, t).start()

            @pl.when(t == GROUP - 1)
            def _():
                out_local(s).start()

    inside_part(0, 8)
    gather_plane(0)
    inside_part(8, 16)
    gather_plane(1)
    inside_part(16, 32)
    give_back(0)
    give_back(1)

    @pl.loop(1, GROUP)
    def _(i):
        gain_landing(i).wait_recv()

    share(0)
    finish(0)
    share(1)
    finish(1)

    for s in range(SETS):
        out_local(s).wait()

        @pl.loop(0, GROUP - 1)
        def _(t):
            out_landing(s, t).wait_recv()

        @pl.loop(0, GROUP - 1)
        def _(t):
            out_copy(s, t).wait_send()

        @pl.loop(0, CHIPS // STEPS)
        def _(g):
            sib_copy(s, g).wait_send()

        @pl.loop(0, CHIPS - 1)
        def _(i):
            fwd_copy(s, i).wait_send()
            back_copy(s, i).wait_send()

        @pl.loop(1, NZ)
        def _(i):
            z_copy(s, i).wait_send()

        pair_copy(s, c).wait_send()

    @pl.loop(1, GROUP)
    def _(i):
        gain_copy(i).wait_send()


def shards(query_rows, key_rows, value_rows, norm_gain):
    tokens, width = query_rows.shape
    heads = width // E
    dma = pltpu.SemaphoreType.DMA
    return pl.pallas_call(
        kernel,
        out_shape=jax.ShapeDtypeStruct((tokens * GROUP, width // GROUP), jnp.bfloat16),
        in_specs=[pl.BlockSpec(memory_space=pl.ANY)] * 3 + [pl.BlockSpec(memory_space=pltpu.VMEM)],
        out_specs=pl.BlockSpec(memory_space=pl.ANY),
        scratch_shapes=[
            pltpu.VMEM((tokens, width), jnp.bfloat16),
            pltpu.VMEM((tokens, width), jnp.bfloat16),
            pltpu.VMEM((tokens, width), jnp.bfloat16),
            pltpu.VMEM((SETS, CHIPS, E, E), jnp.float32),
            pltpu.VMEM((SETS, CHIPS, E, E), jnp.float32),
            pltpu.VMEM((heads, tokens, E), jnp.float32),
            pltpu.VMEM((SETS, CHIPS, PIECE, E), jnp.bfloat16),
            pltpu.VMEM((SETS, CHIPS, PIECE, E), jnp.bfloat16),
            pltpu.VMEM((SETS, CHIPS, PIECE, E), jnp.float32),
            pltpu.VMEM((SETS, PIECE, E), jnp.bfloat16),
            pltpu.VMEM((SETS, NZ, PIECE, E), jnp.bfloat16),
            pltpu.VMEM((SETS, CHIPS, PIECE, E), jnp.bfloat16),
            pltpu.VMEM((SETS, CORES, CHIPS, PIECE, E), jnp.bfloat16),
            pltpu.VMEM((SETS, GROUP, tokens, 2 * E), jnp.bfloat16),
            pltpu.VMEM((8, 4 * E), jnp.float32),
            pltpu.VMEM((GROUP, 8, 4 * E), jnp.float32),
            dma((3,)),
            dma((SETS, CHIPS // STEPS)), dma((SETS, CHIPS // STEPS)),
            dma((SETS, CHIPS)), dma((SETS, CHIPS)),
            dma((SETS, NZ)), dma((SETS, NZ)),
            dma((SETS, CHIPS)), dma((SETS, CHIPS)),
            dma((SETS,)), dma((SETS,)),
            dma((SETS, GROUP)), dma((SETS, GROUP)),
            dma((GROUP,)), dma((GROUP,)),
        ],
        compiler_params=pltpu.CompilerParams(
            collective_id=0, has_side_effects=True, vmem_limit_bytes=48 * 1024 * 1024
        ),
    )(query_rows, key_rows, value_rows, norm_gain.reshape(1, 4 * E))


def solution(mesh):
    placed = (
        P(("seq", "head"), None),
        P(("seq", "head"), None),
        P(("seq", "head"), None),
        P("head"),
    )
    return jax.shard_map(
        shards, mesh=mesh, in_specs=placed, out_specs=P("seq", "head"), check_vma=False
    )
```

time: 265 us -> 70.9 us (0.27)
  waiting for transfers between devices: 128 us -> 0 us
  Pallas kernels: 0 us -> 67.2 us
  local copies, waits for them, and re-layouts: 47.5 us -> 3.59 us
  other arithmetic: 39.6 us -> 0 us
  starting transfers between devices: 17 us -> 0 us
  matrix products: 16.4 us -> 0 us
  between operations: 13.5 us -> 0.01 us
    all_to_all x3 -> x0, waiting for transfers between devices: 68.1 us -> none  [the longest x1 24.4 us: shards(): lax.all_to_all(value_rows, 'head', split_axis=1, concat_axis=0, tiled=True)]
    pallas_call x0 -> x1, Pallas kernels: none -> 67.2 us  [shards(): pl.pallas_call(kernel, out_shape=jax.ShapeDtypeStruct((tokens * GROUP, wi...]
    all_gather x1 -> x0, waiting for transfers between devices: 59.8 us -> none  [entering(): everything = lax.all_gather(value, axis)]
    select_n x32 -> x0, other arithmetic: 33.3 us -> none  [hop(): return jnp.where(reached, new, before)]
    all_to_all x3 -> x0, starting transfers between devices: 17 us -> none  [the longest x1 6.74 us: shards(): lax.all_to_all(key_rows, 'head', split_axis=1, concat_axis=0, tiled=True)]
    dot_general x13 -> x0, matrix products: 16.4 us -> none  [the longest x4 9.01 us: advance(): jnp.einsum('hbc,che->bhe', weights, value_blk, preferred_element_type=jnp...]
    dynamic_slice x12 -> x0, local copies, waits for them, and re-layouts: 12.5 us -> none  [attend(): lax.scan(advance, start_state, (query_blocks, key_blocks, value_blocks))]
    another operation x3 -> x0, local copies, waits for them, and re-layouts: 9.97 us -> none  [the longest x1 3.98 us: attend(): query_blocks = query_heads.reshape(blocks, BLOCK, heads_here, width)]
  transfers between devices with their start and end apart: 4 -> 0, of which waited for: 4 -> 0; matrix products, arithmetic and copies ran while one was open for 7% -> 0% of each run, Pallas kernels for 0% -> 0%
where the time goes in v1:
time: 70.9 us; the launch traced here: 70.8 us
  Pallas kernels  67.2 us (95%)
  local copies, waits for them, and re-layouts  3.59 us (5%)
    pallas_call x1, Pallas kernels, shards(): pl.pallas_call(kernel, out_shape=jax.ShapeDtypeStruct((tokens * GROUP, wi...  67.2 us
    unnamed x5, local copies, waits for them, and re-layouts  3.59 us

profile of v1, /device:TPU:1, one launch (start us, length us, event | category | flops | bytes accessed | tf_op | source)
XLA Modules:
  0.0 70.8 jit_solution(2188663212175358954)
XLA Ops:
  0.0 0.0 copy-start
  0.0 1.6 %copy-done = bf16[256,4096]{1,0:T(8,128)(2,1)S(1)} copy-done((bf16[256,4096]{1,0:T(8,128)(2,1)S(1)}, bf16[256,4096]{1,0:T(8,128)(2,1)}, u32[]{:S(2)}) %copy-start) | copy-done | bytes 2097176
  1.6 0.0 copy-start.1
  1.6 0.7 copy-done.1
  2.3 67.2 %shard_map.46 = bf16[2048,512]{1,0:T(8,128)(2,1)S(1)} custom-call(bf16[256,4096]{1,0:T(8,128)(2,1)S(1)} %copy-done, bf16[256,4096]{1,0:T(8,128)(2,1)} %k_hbm.1, bf16[256,4096]{1,0:T(8,128)(2,1)} %v_hbm.1, f32[1,512]{1,0:T(1,128)S(1)} %bitcast.1), custom_call_target="tpu_custom_call" | custom-call | tf_op jit(solution)/shard_map/pallas_call | solution.py:365
  69.4 1.3 %copy.6 = bf16[2048,512]{1,0:T(8,128)(2,1)} copy(bf16[2048,512]{1,0:T(8,128)(2,1)S(1)} %shard_map.46) | data formatting | bytes 4194304
Async XLA Ops:
  0.0 1.6 %copy-start = (bf16[256,4096]{1,0:T(8,128)(2,1)S(1)}, bf16[256,4096]{1,0:T(8,128)(2,1)}, u32[]{:S(2)}) copy-start(bf16[256,4096]{1,0:T(8,128)(2,1)} %q_hbm.1) | copy-start | bytes 6291460
  1.6 0.7 copy-start.1

commit v2 on v0

v2 whole, which is shorter than its diff:
```python
import jax
import jax.numpy as jnp
from jax import lax
from jax.experimental import pallas as pl
from jax.experimental.pallas import tpu as pltpu
from jax.sharding import PartitionSpec as P

E = 128
TOKENS = 256
HEADS = 32
NX, NY, NZ, CORES = 4, 4, 8, 2
CHIPS = NX * NY
GROUP = NX * CORES
SETS = 4
PER_SET = HEADS // SETS
SUBS = CHIPS // PER_SET
PER_DEST = PER_SET // GROUP
PIECE = E // (SUBS * CORES)
CHUNKS = 4
SCALE = 1024.0
MESH = pl.DeviceIdType.MESH


def encode(state):
    scaled = state * SCALE
    return ((scaled * jnp.abs(scaled)) * (scaled * scaled)).astype(jnp.bfloat16)


def decode(code):
    wide = code.astype(jnp.float32)
    root = lax.rsqrt(lax.rsqrt(jnp.abs(wide))) * (1.0 / SCALE)
    return jnp.where(wide < 0.0, -root, root)


def kernel(q_hbm, k_hbm, v_hbm, gain_hbm, out_hbm,
           q, k, v, own, sib, within, coded, landed, ahead, zcode, zland, pcode, pstate, result, grow, gmine, gall,
           load_sem, own_send, near_recv, rest_recv, fwd_send, fwd_recv, z_send, z_recv, back_send, back_recv,
           pair_send, pair_recv, out_send, out_recv, out_keep, gain_send, gain_recv, z_ready):
    seq, me = lax.axis_index("seq"), lax.axis_index("head")
    z, y = lax.div(seq, NY), lax.rem(seq, NY)
    x, c = lax.div(me, CORES), lax.rem(me, CORES)
    n = y * NX + x
    other = (seq, x * CORES + 1 - c)

    def chip(a):
        return (z * NY + lax.div(a, NX), lax.rem(a, NX) * CORES + c)

    def depth(other_z):
        return (other_z * NY + y, me)

    def turned(i):
        return lax.rem(n + 1 + i, CHIPS)

    def columns(h):
        if isinstance(h, int):
            return pl.ds(h * E, E)
        return pl.ds(pl.multiple_of(h * E, E), E)

    wide = HEADS * E // CHUNKS
    k_loads = [
        pltpu.make_async_copy(k_hbm.at[:, pl.ds(i * wide, wide)], k.at[:, pl.ds(i * wide, wide)], load_sem.at[2 * i])
        for i in range(CHUNKS)
    ]
    v_loads = [
        pltpu.make_async_copy(v_hbm.at[:, pl.ds(i * wide, wide)], v.at[:, pl.ds(i * wide, wide)], load_sem.at[2 * i + 1])
        for i in range(CHUNKS)
    ]
    q_load = pltpu.make_async_copy(q_hbm, q, load_sem.at[2 * CHUNKS])
    gain_load = pltpu.make_async_copy(gain_hbm, grow, load_sem.at[2 * CHUNKS + 1])
    for i in range(CHUNKS):
        k_loads[i].start()
        v_loads[i].start()
    q_load.start()
    gain_load.start()

    barrier = pltpu.get_barrier_semaphore()

    @pl.loop(1, CHIPS)
    def _(i):
        pl.semaphore_signal(barrier, inc=1, device_id=chip(lax.rem(n + i, CHIPS)), device_id_type=MESH)

    @pl.loop(0, NX)
    def _(i):
        pl.semaphore_signal(
            barrier, inc=1, device_id=(seq, lax.rem(x + i, NX) * CORES + 1 - c), device_id_type=MESH
        )

    @pl.loop(z + 1, NZ)
    def _(i):
        pl.semaphore_signal(barrier, inc=1, device_id=depth(i), device_id_type=MESH)

    for i in range(CHUNKS):
        k_loads[i].wait()
        v_loads[i].wait()
        for h in range(i * HEADS // CHUNKS, (i + 1) * HEADS // CHUNKS):
            state = lax.dot_general(
                k[:, columns(h)], v[:, columns(h)], (((0,), (0,)), ((), ())), preferred_element_type=jnp.float32
            )
            dest, place = h // 4, h % 4
            s, a = place // PER_DEST, dest * PER_DEST + place % PER_DEST
            for sub in range(SUBS):
                for core in range(CORES):
                    row = (sub * CORES + core) * PIECE
                    own[s, core, a * SUBS + sub] = state[row:row + PIECE]

    pl.semaphore_wait(barrier, CHIPS - 1 + NX + z)

    @pl.loop(0, z)
    def _(i):
        pl.semaphore_signal(z_ready, inc=1, device_id=depth(i), device_id_type=MESH)

    def near_copy(s, core):
        return pltpu.make_async_remote_copy(
            own.at[s, core], sib.at[s, core], own_send, near_recv.at[s], device_id=other, device_id_type=MESH
        )

    def rest_copy(part, core):
        return pltpu.make_async_remote_copy(
            own.at[part, core], sib.at[part, core], own_send, rest_recv, device_id=other, device_id_type=MESH
        )

    for s in range(SETS):
        near_copy(s, 1 - c).start()
    for s in range(SETS):
        rest_copy(s, c).start()

    def gain_copy(i, src, dst):
        return pltpu.make_async_remote_copy(
            src, dst, gain_send, gain_recv, device_id=(seq, lax.rem(me + i, GROUP)), device_id_type=MESH
        )

    def fwd_copy(s, a, src, dst):
        return pltpu.make_async_remote_copy(
            src, dst, fwd_send, fwd_recv.at[s], device_id=chip(a), device_id_type=MESH
        )

    def z_copy(s, i, src, dst):
        return pltpu.make_async_remote_copy(
            src, dst, z_send, z_recv.at[s], device_id=depth(i), device_id_type=MESH
        )

    def back_copy(s, a, src, dst):
        return pltpu.make_async_remote_copy(
            src, dst, back_send, back_recv.at[s], device_id=chip(a), device_id_type=MESH
        )

    def pair_copy(s, which):
        return pltpu.make_async_remote_copy(
            pstate.at[s, which], pstate.at[s, which], pair_send, pair_recv.at[s],
            device_id=other, device_id_type=MESH,
        )

    def out_place(s, j):
        return out_hbm.at[
            pl.ds(pl.multiple_of(j * TOKENS, TOKENS), TOKENS), pl.ds(s * PER_DEST * E, PER_DEST * E)
        ]

    def out_copy(t, src, dst):
        return pltpu.make_async_remote_copy(
            src, dst, out_send, out_recv, device_id=(seq, lax.rem(me + 1 + t, GROUP)), device_id_type=MESH
        )

    def out_local(part, place):
        return pltpu.make_async_copy(result.at[part, GROUP - 1], place, out_keep)

    most, peers = pl.ds(0, CHIPS - 1), pl.ds(0, GROUP - 1)

    for s in range(SETS):
        near_copy(s, c).wait_recv()

        @pl.loop(0, CHIPS)
        def _(i):
            a = turned(i)
            coded[s, i] = encode(own[s, c, a] + sib[s, c, a])

        @pl.loop(0, CHIPS - 1)
        def _(i):
            fwd_copy(s, turned(i), coded.at[s, i], landed.at[s, n]).start()

        landed[s, n] = coded[s, CHIPS - 1]

    gain_load.wait()
    gmine[...] = jnp.broadcast_to(grow[...], gmine.shape)
    gall[me] = jnp.broadcast_to(grow[...], gmine.shape)

    @pl.loop(1, GROUP)
    def _(i):
        gain_copy(i, gmine, gall.at[me]).start()

    q_load.wait()

    def inside_part(first, last):
        causal = lax.broadcasted_iota(jnp.int32, (TOKENS, TOKENS), 1) <= lax.broadcasted_iota(
            jnp.int32, (TOKENS, TOKENS), 0
        )

        @pl.loop(first // 8, last // 8)
        def _(group):
            for u in range(8):
                h = group * 8 + u
                col = columns(h)
                scores = lax.dot_general(
                    q[:, col], k[:, col], (((1,), (1,)), ((), ())), preferred_element_type=jnp.float32
                )
                weights = jnp.where(causal, scores, 0.0).astype(jnp.bfloat16)
                within[h] = jnp.dot(weights, v[:, col], preferred_element_type=jnp.float32)

    def gather_plane(s):
        fwd_copy(s, n, coded.at[s, most], landed.at[s, most]).wait_recv()
        total = jnp.zeros((PIECE, E), jnp.float32)
        for a in range(CHIPS):
            ahead[s, a] = total
            total = total + decode(landed[s, a])
        zcode[s] = encode(total)
        if s == 0:
            @pl.when(z < NZ - 1)
            def _():
                pl.semaphore_wait(z_ready, NZ - 1 - z)

        @pl.loop(z + 1, NZ)
        def _(i):
            z_copy(s, i, zcode.at[s], zland.at[s, z]).start()

    def give_back(s):
        for count in range(1, NZ):
            @pl.when(z == count)
            def _():
                z_copy(s, z, zland.at[s, pl.ds(0, count)], zland.at[s, pl.ds(0, count)]).wait_recv()

        def add(i, base):
            return base + decode(zland[s, i])

        base = lax.fori_loop(0, z, add, jnp.zeros((PIECE, E), jnp.float32))
        for i in range(CHIPS):
            pcode[s, i] = encode(base + ahead[s, turned(i)])

        @pl.loop(0, CHIPS - 1)
        def _(i):
            back_copy(s, turned(i), pcode.at[s, i], pstate.at[s, c, n]).start()

        pstate[s, c, n] = pcode[s, CHIPS - 1]

    def share(s):
        back_copy(s, n, pcode.at[s, most], pstate.at[s, c, most]).wait_recv()
        pair_copy(s, c).start()

    def finish(s):
        pair_copy(s, 1 - c).wait_recv()
        if s == 0:
            rest_copy(pl.ds(0, SETS), 1 - c).wait_recv()
        for t in range(GROUP):
            j = lax.rem(me + 1 + t, GROUP)
            for u in range(PER_DEST):
                a = j * PER_DEST + u
                place = s * PER_DEST + u
                h = 4 * j + place
                pieces = [(core, a * SUBS + sub) for sub in range(SUBS) for core in range(CORES)]
                before = jnp.concatenate([decode(pstate[s, core, p]) for core, p in pieces], axis=0)
                beside = jnp.concatenate([sib[s, core, p] for core, p in pieces], axis=0)
                before = before + jnp.where(c == 1, beside, 0.0)
                high = before.astype(jnp.bfloat16)
                low = (before - high.astype(jnp.float32)).astype(jnp.bfloat16)
                queries = q[:, columns(h)]
                attended = (
                    within[h]
                    + jnp.dot(queries, high, preferred_element_type=jnp.float32)
                    + jnp.dot(queries, low, preferred_element_type=jnp.float32)
                )
                mean = jnp.mean(attended * attended, axis=-1, keepdims=True)
                gain = gall[j, 0:1, place * E:(place + 1) * E]
                normed = attended * lax.rsqrt(mean + 1e-06) * gain
                result[s, t, :, u * E:(u + 1) * E] = normed.astype(jnp.bfloat16)

        @pl.loop(0, GROUP - 1)
        def _(t):
            out_copy(t, result.at[s, t], out_place(s, me)).start()

        out_local(s, out_place(s, me)).start()

    inside_part(0, 16)
    gather_plane(0)
    inside_part(16, 24)
    gather_plane(1)
    inside_part(24, 32)
    gather_plane(2)
    give_back(0)
    gather_plane(3)
    give_back(1)
    give_back(2)
    give_back(3)
    gain_copy(0, gall.at[peers], gall.at[peers]).wait_recv()
    share(0)
    share(1)
    finish(0)
    share(2)
    finish(1)
    share(3)
    finish(2)
    finish(3)

    rows = pl.ds(0, (GROUP - 1) * TOKENS)
    out_copy(0, out_hbm.at[rows], out_hbm.at[rows]).wait_recv()
    pltpu.make_async_copy(out_hbm.at[pl.ds(0, TOKENS)], out_hbm.at[pl.ds(0, TOKENS)], out_keep).wait()
    out_copy(0, result.at[:, peers], result.at[:, peers]).wait_send()
    pltpu.make_async_remote_copy(own, own, own_send, rest_recv, device_id=other, device_id_type=MESH).wait_send()
    fwd_copy(0, n, coded.at[:, most], coded.at[:, most]).wait_send()
    back_copy(0, n, pcode.at[:, most], pcode.at[:, most]).wait_send()
    for count in range(1, NZ):
        @pl.when(z == NZ - 1 - count)
        def _():
            z_copy(0, z, zland.at[:, pl.ds(0, count)], zland.at[:, pl.ds(0, count)]).wait_send()
    pltpu.make_async_remote_copy(
        pstate.at[:, 0], pstate.at[:, 0], pair_send, pair_recv.at[0], device_id=other, device_id_type=MESH
    ).wait_send()
    gain_copy(0, gall.at[peers], gall.at[peers]).wait_send()


def shards(query_rows, key_rows, value_rows, norm_gain):
    tokens, width = query_rows.shape
    dma = pltpu.SemaphoreType.DMA
    f32, bf16 = jnp.float32, jnp.bfloat16
    held = [pltpu.with_memory_space_constraint(rows, pltpu.HBM) for rows in (query_rows, key_rows, value_rows, norm_gain.reshape(1, 4 * E))]
    return pl.pallas_call(
        kernel,
        out_shape=jax.ShapeDtypeStruct((tokens * GROUP, width // GROUP), bf16),
        in_specs=[pl.BlockSpec(memory_space=pl.ANY)] * 4,
        out_specs=pl.BlockSpec(memory_space=pl.ANY),
        scratch_shapes=[
            pltpu.VMEM((tokens, width), bf16),
            pltpu.VMEM((tokens, width), bf16),
            pltpu.VMEM((tokens, width), bf16),
            pltpu.VMEM((SETS, CORES, CHIPS, PIECE, E), f32),
            pltpu.VMEM((SETS, CORES, CHIPS, PIECE, E), f32),
            pltpu.VMEM((HEADS, tokens, E), f32),
            pltpu.VMEM((SETS, CHIPS, PIECE, E), bf16),
            pltpu.VMEM((SETS, CHIPS, PIECE, E), bf16),
            pltpu.VMEM((SETS, CHIPS, PIECE, E), f32),
            pltpu.VMEM((SETS, PIECE, E), bf16),
            pltpu.VMEM((SETS, NZ, PIECE, E), bf16),
            pltpu.VMEM((SETS, CHIPS, PIECE, E), bf16),
            pltpu.VMEM((SETS, CORES, CHIPS, PIECE, E), bf16),
            pltpu.VMEM((SETS, GROUP, tokens, PER_DEST * E), bf16),
            pltpu.VMEM((1, 4 * E), f32),
            pltpu.VMEM((8, 4 * E), f32),
            pltpu.VMEM((GROUP, 8, 4 * E), f32),
            dma((2 * CHUNKS + 2,)),
            dma, dma((SETS,)), dma,
            dma, dma((SETS,)), dma, dma((SETS,)), dma, dma((SETS,)),
            dma, dma((SETS,)),
            dma, dma, dma, dma, dma,
            pltpu.SemaphoreType.REGULAR,
        ],
        compiler_params=pltpu.CompilerParams(
            collective_id=0, has_side_effects=True, vmem_limit_bytes=48 * 1024 * 1024
        ),
    )(*held)


def solution(mesh):
    placed = (
        P(("seq", "head"), None),
        P(("seq", "head"), None),
        P(("seq", "head"), None),
        P("head"),
    )
    return jax.shard_map(
        shards, mesh=mesh, in_specs=placed, out_specs=P("seq", "head"), check_vma=False
    )
```

time: 265 us -> 50.2 us (0.19)
  waiting for transfers between devices: 128 us -> 0 us
  Pallas kernels: 0 us -> 48.1 us
  local copies, waits for them, and re-layouts: 47.5 us -> 1.32 us
  other arithmetic: 39.6 us -> 0 us
  starting transfers between devices: 17 us -> 0 us
  matrix products: 16.4 us -> 0 us
  between operations: 13.5 us -> 0.01 us
    all_to_all x3 -> x0, waiting for transfers between devices: 68.1 us -> none  [the longest x1 24.4 us: shards(): lax.all_to_all(value_rows, 'head', split_axis=1, concat_axis=0, tiled=True)]
    all_gather x1 -> x0, waiting for transfers between devices: 59.8 us -> none  [entering(): everything = lax.all_gather(value, axis)]
    pallas_call x0 -> x1, Pallas kernels: none -> 48.1 us  [shards(): pl.pallas_call(kernel, out_shape=jax.ShapeDtypeStruct((tokens * GROUP, wi...]
    select_n x32 -> x0, other arithmetic: 33.3 us -> none  [hop(): return jnp.where(reached, new, before)]
    all_to_all x3 -> x0, starting transfers between devices: 17 us -> none  [the longest x1 6.74 us: shards(): lax.all_to_all(key_rows, 'head', split_axis=1, concat_axis=0, tiled=True)]
    dot_general x13 -> x0, matrix products: 16.4 us -> none  [the longest x4 9.01 us: advance(): jnp.einsum('hbc,che->bhe', weights, value_blk, preferred_element_type=jnp...]
    dynamic_slice x12 -> x0, local copies, waits for them, and re-layouts: 12.5 us -> none  [attend(): lax.scan(advance, start_state, (query_blocks, key_blocks, value_blocks))]
    another operation x3 -> x0, local copies, waits for them, and re-layouts: 9.97 us -> none  [the longest x1 3.98 us: attend(): query_blocks = query_heads.reshape(blocks, BLOCK, heads_here, width)]
  transfers between devices with their start and end apart: 4 -> 0, of which waited for: 4 -> 0; matrix products, arithmetic and copies ran while one was open for 7% -> 0% of each run, Pallas kernels for 0% -> 0%
where the time goes in v2:
time: 50.2 us; the launch traced here: 49.5 us
  Pallas kernels  48.1 us (96%)
  local copies, waits for them, and re-layouts  1.32 us (3%)
    pallas_call x1, Pallas kernels, shards(): pl.pallas_call(kernel, out_shape=jax.ShapeDtypeStruct((tokens * GROUP, wi...  48.1 us
    unnamed x1, local copies, waits for them, and re-layouts  1.32 us

profile of v2, /device:TPU:1, one launch (start us, length us, event | category | flops | bytes accessed | tf_op | source)
XLA Modules:
  0.0 49.5 jit_solution(15251410148167380306)
XLA Ops:
  0.0 48.1 %shard_map.46 = bf16[2048,512]{1,0:T(8,128)(2,1)S(1)} custom-call(bf16[256,4096]{1,0:T(8,128)(2,1)} %q_hbm.1, bf16[256,4096]{1,0:T(8,128)(2,1)} %k_hbm.1, bf16[256,4096]{1,0:T(8,128)(2,1)} %v_hbm.1, f32[1,512]{1,0:T(1,128)} %bitcast.1), custom_call_target="tpu_custom_call" | custom-call | tf_op jit(solution)/shard_map/pallas_call | solution.py:323
  48.1 1.3 %copy.6 = bf16[2048,512]{1,0:T(8,128)(2,1)} copy(bf16[2048,512]{1,0:T(8,128)(2,1)S(1)} %shard_map.46) | data formatting | bytes 4194304

commit v3 on v2

v3 whole, which is shorter than its diff:
```python
import jax
import jax.numpy as jnp
from jax import lax
from jax.experimental import pallas as pl
from jax.experimental.pallas import tpu as pltpu
from jax.sharding import PartitionSpec as P

E = 128
TOKENS = 256
HEADS = 32
NX, NY, NZ, CORES = 4, 4, 8, 2
CHIPS = NX * NY
GROUP = NX * CORES
PER_DEVICE = HEADS // GROUP
EVEN, ODD, EVERY = tuple(range(0, GROUP, 2)), tuple(range(1, GROUP, 2)), tuple(range(GROUP))
SETS = ((0, EVEN), (0, ODD), (1, EVERY), (2, EVERY), (3, EVERY))
SIZES = [len(devices) for _, devices in SETS]
SUBS = [CHIPS // size for size in SIZES]
PIECES = [E * size // HEADS for size in SIZES]
ROWS = [slice(sum(PIECES[:s]), sum(PIECES[:s + 1])) for s in range(len(SETS))]
SCALE = 1024.0
MESH = pl.DeviceIdType.MESH


def encode(state):
    scaled = state * SCALE
    return ((scaled * jnp.abs(scaled)) * (scaled * scaled)).astype(jnp.bfloat16)


def decode(code):
    wide = code.astype(jnp.float32)
    root = lax.rsqrt(lax.rsqrt(jnp.abs(wide))) * (1.0 / SCALE)
    return jnp.where(wide < 0.0, -root, root)


def kernel(q_hbm, k_hbm, v_hbm, gain_hbm, out_hbm,
           q, k, v, own, sib, within, coded, landed, ahead, zcode, zland, pcode, pstate, result, grow, gmine, gall,
           load_sem, own_send, near_recv, rest_recv, fwd_send, fwd_recv, z_send, z_recv, back_send, back_recv,
           pair_send, pair_recv, out_send, out_recv, out_keep, gain_send, gain_recv, z_ready):
    seq, me = lax.axis_index("seq"), lax.axis_index("head")
    z, y = lax.div(seq, NY), lax.rem(seq, NY)
    x, c = lax.div(me, CORES), lax.rem(me, CORES)
    n = y * NX + x
    other = (seq, x * CORES + 1 - c)

    def chip(a):
        return (z * NY + lax.div(a, NX), lax.rem(a, NX) * CORES + c)

    def depth(other_z):
        return (other_z * NY + y, me)

    def turned(i):
        return lax.rem(n + 1 + i, CHIPS)

    def columns(h):
        if isinstance(h, int):
            return pl.ds(h * E, E)
        return pl.ds(pl.multiple_of(h * E, E), E)

    def loads(first, width, devices, sems):
        for j in devices:
            part = pl.ds(j * PER_DEVICE * E + first * E, width * E)
            for source, target, sem in ((k_hbm, k, sems[0]), (v_hbm, v, sems[1])):
                pltpu.make_async_copy(source.at[:, part], target.at[:, part], load_sem.at[sem]).start()

    def loaded(width, devices, sems):
        part = pl.ds(0, width * len(devices) * E)
        for source, target, sem in ((k_hbm, k, sems[0]), (v_hbm, v, sems[1])):
            pltpu.make_async_copy(source.at[:, part], target.at[:, part], load_sem.at[sem]).wait()

    q_load = pltpu.make_async_copy(q_hbm, q, load_sem.at[6])
    gain_load = pltpu.make_async_copy(gain_hbm, grow, load_sem.at[7])
    loads(0, 1, EVEN, (0, 1))
    loads(0, 4, ODD, (2, 3))
    loads(1, 3, EVEN, (4, 5))
    zland[...] = jnp.zeros_like(zland)

    barrier = pltpu.get_barrier_semaphore()

    @pl.loop(1, CHIPS)
    def _(i):
        pl.semaphore_signal(barrier, inc=1, device_id=chip(lax.rem(n + i, CHIPS)), device_id_type=MESH)

    @pl.loop(0, NX)
    def _(i):
        pl.semaphore_signal(
            barrier, inc=1, device_id=(seq, lax.rem(x + i, NX) * CORES + 1 - c), device_id_type=MESH
        )

    @pl.loop(z + 1, NZ)
    def _(i):
        pl.semaphore_signal(barrier, inc=1, device_id=depth(i), device_id_type=MESH)

    q_load.start()
    gain_load.start()

    def outer(s, a):
        place, devices = SETS[s]
        col = columns(devices[a] * PER_DEVICE + place)
        state = lax.dot_general(k[:, col], v[:, col], (((0,), (0,)), ((), ())), preferred_element_type=jnp.float32)
        for sub in range(SUBS[s]):
            for core in range(CORES):
                row = (sub * CORES + core) * PIECES[s]
                own[core, a * SUBS[s] + sub, ROWS[s]] = state[row:row + PIECES[s]]

    def own_copy(s, core, sem):
        part = (core, slice(None), ROWS[s])
        return pltpu.make_async_remote_copy(
            own.at[part], sib.at[part], own_send, sem, device_id=other, device_id_type=MESH
        )

    def gain_copy(i, src, dst):
        return pltpu.make_async_remote_copy(
            src, dst, gain_send, gain_recv, device_id=(seq, lax.rem(me + i, GROUP)), device_id_type=MESH
        )

    def fwd_copy(s, a, src, dst):
        return pltpu.make_async_remote_copy(
            src, dst, fwd_send, fwd_recv.at[s], device_id=chip(a), device_id_type=MESH
        )

    def z_copy(s, i, src, dst):
        return pltpu.make_async_remote_copy(
            src, dst, z_send, z_recv.at[s], device_id=depth(i), device_id_type=MESH
        )

    def back_copy(s, a, src, dst):
        return pltpu.make_async_remote_copy(
            src, dst, back_send, back_recv.at[s], device_id=chip(a), device_id_type=MESH
        )

    def pair_copy(s, which):
        part = (which, slice(None), ROWS[s])
        return pltpu.make_async_remote_copy(
            pstate.at[part], pstate.at[part], pair_send, pair_recv.at[s], device_id=other, device_id_type=MESH
        )

    def out_place(place, j):
        return out_hbm.at[pl.ds(pl.multiple_of(j * TOKENS, TOKENS), TOKENS), pl.ds(place * E, E)]

    def out_copy(j, src, dst):
        return pltpu.make_async_remote_copy(src, dst, out_send, out_recv, device_id=(seq, j), device_id_type=MESH)

    most, peers = pl.ds(0, CHIPS - 1), pl.ds(0, GROUP - 1)

    def outers(s):
        for a in range(SIZES[s]):
            outer(s, a)

    def send_near(s):
        own_copy(s, 1 - c, near_recv.at[s]).start()

    def forward(s):
        own_copy(s, c, near_recv.at[s]).wait_recv()
        rows = ROWS[s]
        for i in range(CHIPS):
            a = turned(i)
            coded[i, rows] = encode(own[c, a, rows] + sib[c, a, rows])

        @pl.loop(0, CHIPS - 1)
        def _(i):
            fwd_copy(s, turned(i), coded.at[i, rows], landed.at[n, rows]).start()

        landed[n, rows] = coded[CHIPS - 1, rows]

    def share_gain():
        gain_load.wait()
        gmine[...] = jnp.broadcast_to(grow[...], gmine.shape)
        gall[me] = jnp.broadcast_to(grow[...], gmine.shape)

        @pl.loop(1, GROUP)
        def _(i):
            gain_copy(i, gmine, gall.at[me]).start()

    def inside_part(first, last):
        causal = lax.broadcasted_iota(jnp.int32, (TOKENS, TOKENS), 1) <= lax.broadcasted_iota(
            jnp.int32, (TOKENS, TOKENS), 0
        )

        @pl.loop(first // 8, last // 8)
        def _(group):
            for u in range(8):
                h = group * 8 + u
                col = columns(h)
                scores = lax.dot_general(
                    q[:, col], k[:, col], (((1,), (1,)), ((), ())), preferred_element_type=jnp.float32
                )
                weights = jnp.where(causal, scores, 0.0).astype(jnp.bfloat16)
                within[h] = jnp.dot(weights, v[:, col], preferred_element_type=jnp.float32)

    def gather_plane(s):
        rows = ROWS[s]
        fwd_copy(s, n, coded.at[most, rows], landed.at[most, rows]).wait_recv()
        total = jnp.zeros((PIECES[s], E), jnp.float32)
        for a in range(CHIPS):
            ahead[a, rows] = total
            total = total + decode(landed[a, rows])
        zcode[rows] = encode(total)
        if s == 0:
            @pl.when(z < NZ - 1)
            def _():
                pl.semaphore_wait(z_ready, NZ - 1 - z)

        @pl.loop(z + 1, NZ)
        def _(i):
            z_copy(s, i, zcode.at[rows], zland.at[z, rows]).start()

    def give_back(s):
        rows = ROWS[s]
        for count in range(1, NZ):
            @pl.when(z == count)
            def _():
                earlier = zland.at[pl.ds(0, count), rows]
                z_copy(s, z, earlier, earlier).wait_recv()

        base = decode(zland[0, rows])
        for i in range(1, NZ - 1):
            base = base + decode(zland[i, rows])
        for i in range(CHIPS):
            pcode[i, rows] = encode(base + ahead[turned(i), rows])

        @pl.loop(0, CHIPS - 1)
        def _(i):
            back_copy(s, turned(i), pcode.at[i, rows], pstate.at[c, n, rows]).start()

        pstate[c, n, rows] = pcode[CHIPS - 1, rows]

    def share(s):
        rows = ROWS[s]
        back_copy(s, n, pcode.at[most, rows], pstate.at[c, most, rows]).wait_recv()
        pair_copy(s, c).start()

    def finish(s):
        pair_copy(s, 1 - c).wait_recv()
        rows = ROWS[s]
        place, devices = SETS[s]
        if s == 0:
            everything = sib.at[1 - c]
            pltpu.make_async_remote_copy(
                everything, everything, own_send, rest_recv, device_id=other, device_id_type=MESH
            ).wait_recv()
        for t in range(SIZES[s]):
            a = lax.rem(x * SIZES[s] // NX + 1 + t, SIZES[s])
            j = a * (GROUP // SIZES[s]) + devices[0]
            h = j * PER_DEVICE + place
            pieces = [(core, a * SUBS[s] + sub) for sub in range(SUBS[s]) for core in range(CORES)]
            before = jnp.concatenate([decode(pstate[core, p, rows]) for core, p in pieces], axis=0)
            beside = jnp.concatenate([sib[core, p, rows] for core, p in pieces], axis=0)
            before = before + jnp.where(c == 1, beside, 0.0)
            high = before.astype(jnp.bfloat16)
            low = (before - high.astype(jnp.float32)).astype(jnp.bfloat16)
            queries = q[:, columns(h)]
            attended = (
                within[h]
                + jnp.dot(queries, high, preferred_element_type=jnp.float32)
                + jnp.dot(queries, low, preferred_element_type=jnp.float32)
            )
            mean = jnp.mean(attended * attended, axis=-1, keepdims=True)
            gain = gall[j, 0:1, place * E:(place + 1) * E]
            normed = attended * lax.rsqrt(mean + 1e-06) * gain
            result[j, :, place * E:(place + 1) * E] = normed.astype(jnp.bfloat16)

        @pl.loop(0, SIZES[s])
        def _(t):
            a = lax.rem(x * SIZES[s] // NX + 1 + t, SIZES[s])
            j = a * (GROUP // SIZES[s]) + devices[0]
            ready = result.at[j, :, pl.ds(place * E, E)]

            @pl.when(j != me)
            def _():
                out_copy(j, ready, out_place(place, me)).start()

            @pl.when(j == me)
            def _():
                pltpu.make_async_copy(ready, out_place(place, me), out_keep).start()

    loaded(1, EVEN, (0, 1))
    outers(0)
    pl.semaphore_wait(barrier, CHIPS - 1 + NX + z)
    send_near(0)

    @pl.loop(0, z)
    def _(i):
        pl.semaphore_signal(z_ready, inc=1, device_id=depth(i), device_id_type=MESH)

    loaded(4, ODD, (2, 3))
    outers(1)
    send_near(1)
    loaded(3, EVEN, (4, 5))
    outers(2)
    send_near(2)
    forward(0)
    outers(3)
    send_near(3)
    forward(1)
    outers(4)
    send_near(4)
    forward(2)
    forward(3)
    forward(4)
    q_load.wait()
    inside_part(0, 8)
    gather_plane(0)
    share_gain()
    inside_part(8, 16)
    gather_plane(1)
    inside_part(16, 24)
    gather_plane(2)
    give_back(0)
    for s in range(len(SETS)):
        own_copy(s, c, rest_recv).start()
    inside_part(24, 32)
    gather_plane(3)
    give_back(1)
    gather_plane(4)
    give_back(2)
    give_back(3)
    give_back(4)
    gain_copy(0, gall.at[peers], gall.at[peers]).wait_recv()
    share(0)
    finish(0)
    share(1)
    finish(1)
    share(2)
    finish(2)
    share(3)
    finish(3)
    share(4)
    finish(4)

    arrived = out_hbm.at[pl.ds(0, (GROUP - 1) * TOKENS)]
    out_copy(me, arrived, arrived).wait_recv()
    kept = out_hbm.at[pl.ds(0, TOKENS)]
    pltpu.make_async_copy(kept, kept, out_keep).wait()
    out_copy(me, result.at[peers], result.at[peers]).wait_send()
    pltpu.make_async_remote_copy(own, own, own_send, rest_recv, device_id=other, device_id_type=MESH).wait_send()
    fwd_copy(0, n, coded.at[most], coded.at[most]).wait_send()
    back_copy(0, n, pcode.at[most], pcode.at[most]).wait_send()
    for count in range(1, NZ):
        @pl.when(z == NZ - 1 - count)
        def _():
            z_copy(0, z, zland.at[pl.ds(0, count)], zland.at[pl.ds(0, count)]).wait_send()
    pltpu.make_async_remote_copy(
        pstate.at[0], pstate.at[0], pair_send, pair_recv.at[0], device_id=other, device_id_type=MESH
    ).wait_send()
    gain_copy(0, gall.at[peers], gall.at[peers]).wait_send()


def shards(query_rows, key_rows, value_rows, norm_gain):
    tokens, width = query_rows.shape
    dma, per_set = pltpu.SemaphoreType.DMA, pltpu.SemaphoreType.DMA((len(SETS),))
    f32, bf16 = jnp.float32, jnp.bfloat16
    held = [
        pltpu.with_memory_space_constraint(rows, pltpu.HBM)
        for rows in (query_rows, key_rows, value_rows, norm_gain.reshape(1, PER_DEVICE * E))
    ]
    return pl.pallas_call(
        kernel,
        out_shape=jax.ShapeDtypeStruct((tokens * GROUP, width // GROUP), bf16),
        in_specs=[pl.BlockSpec(memory_space=pl.ANY)] * 4,
        out_specs=pl.BlockSpec(memory_space=pl.ANY),
        scratch_shapes=[
            pltpu.VMEM((tokens, width), bf16),
            pltpu.VMEM((tokens, width), bf16),
            pltpu.VMEM((tokens, width), bf16),
            pltpu.VMEM((CORES, CHIPS, E, E), f32),
            pltpu.VMEM((CORES, CHIPS, E, E), f32),
            pltpu.VMEM((HEADS, tokens, E), f32),
            pltpu.VMEM((CHIPS, E, E), bf16),
            pltpu.VMEM((CHIPS, E, E), bf16),
            pltpu.VMEM((CHIPS, E, E), f32),
            pltpu.VMEM((E, E), bf16),
            pltpu.VMEM((NZ, E, E), bf16),
            pltpu.VMEM((CHIPS, E, E), bf16),
            pltpu.VMEM((CORES, CHIPS, E, E), bf16),
            pltpu.VMEM((GROUP, tokens, PER_DEVICE * E), bf16),
            pltpu.VMEM((1, PER_DEVICE * E), f32),
            pltpu.VMEM((8, PER_DEVICE * E), f32),
            pltpu.VMEM((GROUP, 8, PER_DEVICE * E), f32),
            dma((8,)), dma, per_set, dma, dma, per_set, dma, per_set, dma, per_set, dma, per_set,
            dma, dma, dma, dma, dma,
            pltpu.SemaphoreType.REGULAR,
        ],
        compiler_params=pltpu.CompilerParams(
            collective_id=0, has_side_effects=True, vmem_limit_bytes=48 * 1024 * 1024
        ),
    )(*held)


def solution(mesh):
    placed = (
        P(("seq", "head"), None),
        P(("seq", "head"), None),
        P(("seq", "head"), None),
        P("head"),
    )
    return jax.shard_map(
        shards, mesh=mesh, in_specs=placed, out_specs=P("seq", "head"), check_vma=False
    )
```

time: 50.2 us -> 49.1 us (0.978)
  Pallas kernels: 48.1 us -> 47.4 us
    pallas_call x1, Pallas kernels: 48.1 us -> 47.4 us  [shards(): pl.pallas_call(kernel, out_shape=jax.ShapeDtypeStruct((tokens * GROUP, wi...]
where the time goes in v3:
time: 49.1 us; the launch traced here: 48.7 us
  Pallas kernels  47.4 us (97%)
  local copies, waits for them, and re-layouts  1.32 us (3%)
    pallas_call x1, Pallas kernels, shards(): pl.pallas_call(kernel, out_shape=jax.ShapeDtypeStruct((tokens * GROUP, wi...  47.4 us
    unnamed x1, local copies, waits for them, and re-layouts  1.32 us

profile of v3, /device:TPU:1, one launch (start us, length us, event | category | flops | bytes accessed | tf_op | source)
XLA Modules:
  0.0 48.7 jit_solution(1267316118051902536)
XLA Ops:
  0.0 47.4 %shard_map.46 = bf16[2048,512]{1,0:T(8,128)(2,1)S(1)} custom-call(bf16[256,4096]{1,0:T(8,128)(2,1)} %q_hbm.1, bf16[256,4096]{1,0:T(8,128)(2,1)} %k_hbm.1, bf16[256,4096]{1,0:T(8,128)(2,1)} %v_hbm.1, f32[1,512]{1,0:T(1,128)} %bitcast.1), custom_call_target="tpu_custom_call" | custom-call | tf_op jit(solution)/shard_map/pallas_call | solution.py:357
  47.4 1.3 %copy.6 = bf16[2048,512]{1,0:T(8,128)(2,1)} copy(bf16[2048,512]{1,0:T(8,128)(2,1)S(1)} %shard_map.46) | data formatting | bytes 4194304

commit v4 on v3

--- a/solution.py
+++ b/solution.py
@@ -70,11 +70,6 @@
 
     q_load = pltpu.make_async_copy(q_hbm, q, load_sem.at[6])
     gain_load = pltpu.make_async_copy(gain_hbm, grow, load_sem.at[7])
-    loads(0, 1, EVEN, (0, 1))
-    loads(0, 4, ODD, (2, 3))
-    loads(1, 3, EVEN, (4, 5))
-    zland[...] = jnp.zeros_like(zland)
-
     barrier = pltpu.get_barrier_semaphore()
 
     @pl.loop(1, CHIPS)
@@ -87,9 +82,14 @@
             barrier, inc=1, device_id=(seq, lax.rem(x + i, NX) * CORES + 1 - c), device_id_type=MESH
         )
 
+    loads(0, 1, EVEN, (0, 1))
+    loads(0, 4, ODD, (2, 3))
+    loads(1, 3, EVEN, (4, 5))
     @pl.loop(z + 1, NZ)
     def _(i):
         pl.semaphore_signal(barrier, inc=1, device_id=depth(i), device_id_type=MESH)
+
+    zland[...] = jnp.zeros_like(zland)
 
     q_load.start()
     gain_load.start()
@@ -310,10 +310,10 @@
     for s in range(len(SETS)):
         own_copy(s, c, rest_recv).start()
     inside_part(24, 32)
+    give_back(1)
     gather_plane(3)
-    give_back(1)
+    give_back(2)
     gather_plane(4)
-    give_back(2)
     give_back(3)
     give_back(4)
     gain_copy(0, gall.at[peers], gall.at[peers]).wait_recv()

time: 49.1 us -> 49.1 us (level)
  no operation moved by 1% of the time
where the time goes in v4:
time: 49.1 us; the launch traced here: 48.5 us
  Pallas kernels  47.1 us (96%)
  local copies, waits for them, and re-layouts  1.32 us (3%)
    pallas_call x1, Pallas kernels, shards(): pl.pallas_call(kernel, out_shape=jax.ShapeDtypeStruct((tokens * GROUP, wi...  47.1 us
    unnamed x1, local copies, waits for them, and re-layouts  1.32 us

profile of v4, /device:TPU:1, one launch (start us, length us, event | category | flops | bytes accessed | tf_op | source)
XLA Modules:
  0.0 48.5 jit_solution(15278632871853733560)
XLA Ops:
  0.0 47.1 %shard_map.46 = bf16[2048,512]{1,0:T(8,128)(2,1)S(1)} custom-call(bf16[256,4096]{1,0:T(8,128)(2,1)} %q_hbm.1, bf16[256,4096]{1,0:T(8,128)(2,1)} %k_hbm.1, bf16[256,4096]{1,0:T(8,128)(2,1)} %v_hbm.1, f32[1,512]{1,0:T(1,128)} %bitcast.1), custom_call_target="tpu_custom_call" | custom-call | tf_op jit(solution)/shard_map/pallas_call | solution.py:357
  47.1 1.3 %copy.6 = bf16[2048,512]{1,0:T(8,128)(2,1)} copy(bf16[2048,512]{1,0:T(8,128)(2,1)S(1)} %shard_map.46) | data formatting | bytes 4194304

commit v5 on v4

--- a/solution.py
+++ b/solution.py
@@ -50,7 +50,7 @@
         return (other_z * NY + y, me)
 
     def turned(i):
-        return lax.rem(n + 1 + i, CHIPS)
+        return lax.rem(n + 1 + i + c * (CHIPS - 2 - 2 * i), CHIPS)
 
     def columns(h):
         if isinstance(h, int):
@@ -230,6 +230,23 @@
         back_copy(s, n, pcode.at[most, rows], pstate.at[c, most, rows]).wait_recv()
         pair_copy(s, c).start()
 
+    def target(s, t):
+        per_chip = SIZES[s] // NX
+        step = (1, 3, 1, 3, 2, 2, 0, 0)[t] if per_chip == 2 else (1, 3, 2, 0)[t]
+        bit = (0, 0, 1, 1, 0, 1, 0, 1)[t] if per_chip == 2 else 0
+        dest = lax.rem(x + step + c * ((NX - 2 * step) if step % 2 else 0), NX)
+        a = dest * per_chip + bit
+        return a, a * (GROUP // SIZES[s]) + SETS[s][1][0]
+
+    def keep_or_send(j, ready, place):
+        @pl.when(j != me)
+        def _():
+            out_copy(j, ready, out_place(place, me)).start()
+
+        @pl.when(j == me)
+        def _():
+            pltpu.make_async_copy(ready, out_place(place, me), out_keep).start()
+
     def finish(s):
         pair_copy(s, 1 - c).wait_recv()
         rows = ROWS[s]
@@ -240,8 +257,7 @@
                 everything, everything, own_send, rest_recv, device_id=other, device_id_type=MESH
             ).wait_recv()
         for t in range(SIZES[s]):
-            a = lax.rem(x * SIZES[s] // NX + 1 + t, SIZES[s])
-            j = a * (GROUP // SIZES[s]) + devices[0]
+            a, j = target(s, t)
             h = j * PER_DEVICE + place
             pieces = [(core, a * SUBS[s] + sub) for sub in range(SUBS[s]) for core in range(CORES)]
             before = jnp.concatenate([decode(pstate[core, p, rows]) for core, p in pieces], axis=0)
@@ -260,19 +276,13 @@
             normed = attended * lax.rsqrt(mean + 1e-06) * gain
             result[j, :, place * E:(place + 1) * E] = normed.astype(jnp.bfloat16)
 
-        @pl.loop(0, SIZES[s])
-        def _(t):
-            a = lax.rem(x * SIZES[s] // NX + 1 + t, SIZES[s])
-            j = a * (GROUP // SIZES[s]) + devices[0]
+        for t in range(SIZES[s]):
+            _, j = target(s, t)
             ready = result.at[j, :, pl.ds(place * E, E)]
-
-            @pl.when(j != me)
-            def _():
+            if t < SIZES[s] - SIZES[s] // NX:
                 out_copy(j, ready, out_place(place, me)).start()
-
-            @pl.when(j == me)
-            def _():
-                pltpu.make_async_copy(ready, out_place(place, me), out_keep).start()
+            else:
+                keep_or_send(j, ready, place)
 
     loaded(1, EVEN, (0, 1))
     outers(0)

time: 49.1 us -> 48.9 us (level)
  no operation moved by 1% of the time
where the time goes in v5:
time: 48.9 us; the launch traced here: 48.3 us
  Pallas kernels  47 us (96%)
  local copies, waits for them, and re-layouts  1.32 us (3%)
    pallas_call x1, Pallas kernels, shards(): pl.pallas_call(kernel, out_shape=jax.ShapeDtypeStruct((tokens * GROUP, wi...  47 us
    unnamed x1, local copies, waits for them, and re-layouts  1.32 us

profile of v5, /device:TPU:1, one launch (start us, length us, event | category | flops | bytes accessed | tf_op | source)
XLA Modules:
  0.0 48.3 jit_solution(9201885105064479893)
XLA Ops:
  0.0 47.0 %shard_map.46 = bf16[2048,512]{1,0:T(8,128)(2,1)S(1)} custom-call(bf16[256,4096]{1,0:T(8,128)(2,1)} %q_hbm.1, bf16[256,4096]{1,0:T(8,128)(2,1)} %k_hbm.1, bf16[256,4096]{1,0:T(8,128)(2,1)} %v_hbm.1, f32[1,512]{1,0:T(1,128)} %bitcast.1), custom_call_target="tpu_custom_call" | custom-call | tf_op jit(solution)/shard_map/pallas_call | solution.py:367
  47.0 1.3 %copy.6 = bf16[2048,512]{1,0:T(8,128)(2,1)} copy(bf16[2048,512]{1,0:T(8,128)(2,1)S(1)} %shard_map.46) | data formatting | bytes 4194304
